TPU v7x, 32 devices: a whole 2x2x4 slice. The times are simulated.
32 devices in a mesh: span: 4 (over y, core), seq: 8 (over z, x).
Axes of the slice: x: 2, y: 2, z: 4, core: 2. Of those that a mesh axis runs over, the one named last changes fastest.
Arguments:
- qkv: bfloat16 [3, 4, 512, 2048], P(None, 'span', 'seq'), may hold values from -6 to 6
- lengths: int32 [4], replicated, may hold values from 256 to 512, as said below
Outputs:
- attended: bfloat16 [4, 512, 2048], P('span', 'seq')
Inputs may be any that keep to these rules, and one draw needn't show every extreme that they name: `lengths`: the live tokens of a span are its first ones; some span is full.
All inputs are finite; a program needn't handle non-finite values.
Results may differ from a plain program's by a relative error of at most 0.0065.
Values may be sent and summed in bfloat16 or wider, within the bound.
A program may use at most 64 MiB of HBM per device.

v0:
```python
import jax
import jax.numpy as jnp
from jax import lax
from jax.sharding import PartitionSpec as P

HD = 128


masked_fill = -1e30


def block_terms(queries, key_rows, values, key_live):
    scores = jnp.einsum(
        "hqe,hke->hqk", queries, key_rows, preferred_element_type=jnp.float32
    ) * key_rows.shape[-1] ** (-0.5)
    scores = jnp.where(key_live[None, None, :], scores, masked_fill)
    row_peak = jnp.max(scores, axis=-1)
    weights = jnp.where(key_live[None, None, :], jnp.exp(scores - row_peak[..., None]), 0.0).astype(
        jnp.bfloat16
    )
    numerator = jnp.einsum("hqk,hke->hqe", weights, values, preferred_element_type=jnp.float32)
    weight_sum = jnp.sum(weights.astype(jnp.float32), axis=-1)
    return (row_peak, numerator, weight_sum)


def combine(first_terms, second_terms):
    row_peak = jnp.maximum(first_terms[0], second_terms[0])
    scale_first = jnp.exp(first_terms[0] - row_peak)
    scale_second = jnp.exp(second_terms[0] - row_peak)
    numerator = first_terms[1] * scale_first[..., None] + second_terms[1] * scale_second[..., None]
    weight_sum = first_terms[2] * scale_first + second_terms[2] * scale_second
    return (row_peak, numerator, weight_sum)


def shards(qkv, lengths):
    span_index = lax.axis_index("span")
    spread = lax.all_to_all(qkv, "seq", split_axis=3, concat_axis=2, tiled=True)
    query_part = spread[0:1]
    pair_part = spread[1:3]
    span_rows = query_part.shape[2]
    heads_here = query_part.shape[3] // HD

    def split_heads(stacked):
        return stacked.reshape(stacked.shape[0], span_rows, heads_here, HD).transpose(0, 2, 1, 3)

    queries = split_heads(query_part)[0]
    pair_heads = split_heads(pair_part)
    positions = jnp.arange(span_rows)
    span_list = jnp.arange(lengths.shape[0])

    def live_keys(other_index):
        live_count = jnp.sum(jnp.where(span_list == other_index, lengths, 0))
        return (other_index <= span_index) & (positions < live_count)

    initial = (
        jnp.full((heads_here, span_rows), masked_fill, jnp.float32),
        jnp.zeros((heads_here, span_rows, HD), jnp.float32),
        jnp.zeros((heads_here, span_rows), jnp.float32),
    )
    arrived_block = lax.all_gather(pair_heads, "span", axis=2, tiled=True)
    blocks = arrived_block.shape[2] // span_rows
    first_span = jnp.int32(0) // span_rows
    lower_block = jnp.clip(-first_span, 0, blocks)
    upper_block = jnp.clip(span_index + 1, 0, blocks)

    def add_single(block_number, current):
        block_part = lax.dynamic_slice_in_dim(arrived_block, block_number * span_rows, span_rows, 2)
        return combine(
            current, block_terms(queries, block_part[0], block_part[1], live_keys(block_number))
        )

    running_state = lax.fori_loop(lower_block, upper_block, add_single, initial)
    attended = running_state[1] / running_state[2][..., None]
    own_count = jnp.sum(jnp.where(span_list == span_index, lengths, 0))
    attended = jnp.where((positions < own_count)[None, :, None], attended, 0.0).astype(jnp.bfloat16)
    merged = attended.transpose(1, 0, 2).reshape(1, span_rows, heads_here * HD)
    return lax.all_to_all(merged, "seq", split_axis=1, concat_axis=2, tiled=True)


def solution(mesh):
    in_specs = (P(None, "span", "seq", None), P())
    out_specs = P("span", "seq", None)
    return jax.shard_map(shards, mesh=mesh, in_specs=in_specs, out_specs=out_specs, check_vma=False)
```

profile of v0, /device:TPU:5, one launch (start us, length us, event | category | flops | bytes accessed | tf_op | source)
XLA Modules:
  0.0 105.3 jit_solution(9917762800228693500)
XLA Ops:
  6.5 0.0 all-gather.2.cloned.1.call-start
  6.5 2.8 %copy.40 = bf16[3,1,64,2048]{2,0,1,3:T(4,128)(2,1)S(1)} copy(bf16[3,1,64,2048]{3,2,1,0:T(8,128)(2,1)} %param.4) | data formatting | bytes 1572864 | tf_op args[0]
  9.4 1.4 %reshape.28 = bf16[8,2,24576]{2,1,0:T(2,128)(2,1)S(1)} reshape(bf16[2048,1,3,64]{3,2,1,0:T(4,128)(2,1)S(1)} %bitcast.55) | data formatting | bytes 1572864
  10.8 24.7 %all_to_all.33 = bf16[8,2,24576]{2,1,0:T(2,128)(2,1)} all-to-all(bf16[8,2,24576]{2,1,0:T(2,128)(2,1)S(1)} %reshape.28), channel_id=1, replica_groups=mesh['span'=4,'seq'=8] {'seq'}, dimensions={0} | all-to-all | bytes 1572864 | tf_op jit(solution)/shard_map/all_to_all | solution.py:37
  35.6 2.9 %reshape.29 = bf16[2048,1,3,64]{3,2,1,0:T(4,128)(2,1)S(1)} reshape(bf16[8,2,24576]{2,1,0:T(2,128)(2,1)} %all_to_all.33) | data formatting | bytes 1572864
  38.5 1.2 %copy.51 = bf16[3,1,64,8,256]{4,3,2,0,1:T(8,128)(2,1)S(1)} copy(bf16[3,1,64,8,256]{2,0,4,3,1:T(4,128)(2,1)S(1)} %bitcast.54) | data formatting | bytes 1572864 | tf_op jit(solution)/shard_map/all_to_all | solution.py:37
  39.7 0.0 copy-start
  39.7 0.1 copy.42
  39.8 0.9 reshape.25
  40.8 0.0 all-gather.2.cloned.1.call-update
  40.8 0.6 fusion.11
  41.4 0.6 iota_compare_fusion.1
  42.1 0.1 reshape.26
  42.2 20.7 %all-gather.2.cloned.1.call-done = bf16[2,2,2048,128]{3,1,2,0:T(2,128)(2,1)} async-done(((bf16[2,2,512,128]{3,1,2,0:T(2,128)(2,1)}), bf16[2,2,2048,128]{3,1,2,0:T(2,128)(2,1)}) %all-gather.2.cloned.1.call-update) | async-done | bytes 2097168 | tf_op jit(solution)/shard_map/all_gather | solution.py:60
  63.0 18.6 %while.15 = (s32[]{:T(128)}, f32[2,512]{1,0:T(2,128)S(1)}, f32[2,512,128]{2,1,0:T(8,128)S(1)}, f32[2,512]{1,0:T(2,128)S(1)}, s32[]{:T(128)}, /*index=5*/s32[]{:T...) while((s32[]{:T(128)}, f32[2,512]{1,0:T(2,128)S(1)}, ...), condition=%wide.region_5.6_spmd.clone, body=%wide.region_1.0_spmd.clone.sunk | while | flops 274076672 | bytes 9230061 | solution.py:72
  63.0 1.4 %constant_dynamic-slice_fusion.3 = (bf16[1,2,512,128]{3,1,2,0:T(2,128)(2,1)S(1)}, bf16[1,2,512,128]{3,1,2,0:T(2,128)(2,1)S(1)}) fusion(bf16[2,2,2048,128]{3,1,2,0:T(2,128)(2,1)} %get-tuple-element.272, s32[]{:T(128)S(6)} %add.33, s32[]{:T(128)S(6)} %select_n.57), kind=kLoop, calls=%fused_computation.22.clone.1 | loop fusion | bytes 1048584 | tf_op jit(solution)/shard_map/while/body/slice | solution.py:69
  64.4 0.6 fusion.22
  65.0 0.6 fusion.23
  65.6 0.5 bitcast_reduce_fusion.2
  66.1 0.6 convert_reduce_fusion.2
  66.8 0.8 fusion.24
  67.6 1.4 %constant_dynamic-slice_fusion.3 = (bf16[1,2,512,128]{3,1,2,0:T(2,128)(2,1)S(1)}, bf16[1,2,512,128]{3,1,2,0:T(2,128)(2,1)S(1)}) fusion(bf16[2,2,2048,128]{3,1,2,0:T(2,128)(2,1)} %get-tuple-element.272, s32[]{:T(128)S(6)} %add.33, s32[]{:T(128)S(6)} %select_n.57), kind=kLoop, calls=%fused_computation.22.clone.1 | loop fusion | bytes 1048584 | tf_op jit(solution)/shard_map/while/body/slice | solution.py:69
  69.0 0.6 fusion.22
  69.7 0.6 fusion.23
  70.3 0.5 bitcast_reduce_fusion.2
  70.8 0.6 convert_reduce_fusion.2
  71.4 0.8 fusion.24
  72.3 1.4 %constant_dynamic-slice_fusion.3 = (bf16[1,2,512,128]{3,1,2,0:T(2,128)(2,1)S(1)}, bf16[1,2,512,128]{3,1,2,0:T(2,128)(2,1)S(1)}) fusion(bf16[2,2,2048,128]{3,1,2,0:T(2,128)(2,1)} %get-tuple-element.272, s32[]{:T(128)S(6)} %add.33, s32[]{:T(128)S(6)} %select_n.57), kind=kLoop, calls=%fused_computation.22.clone.1 | loop fusion | bytes 1048584 | tf_op jit(solution)/shard_map/while/body/slice | solution.py:69
  73.7 0.6 fusion.22
  74.3 0.6 fusion.23
  75.0 0.5 bitcast_reduce_fusion.2
  75.4 0.6 convert_reduce_fusion.2
  76.1 0.8 fusion.24
  76.9 1.4 %constant_dynamic-slice_fusion.3 = (bf16[1,2,512,128]{3,1,2,0:T(2,128)(2,1)S(1)}, bf16[1,2,512,128]{3,1,2,0:T(2,128)(2,1)S(1)}) fusion(bf16[2,2,2048,128]{3,1,2,0:T(2,128)(2,1)} %get-tuple-element.272, s32[]{:T(128)S(6)} %add.33, s32[]{:T(128)S(6)} %select_n.57), kind=kLoop, calls=%fused_computation.22.clone.1 | loop fusion | bytes 1048584 | tf_op jit(solution)/shard_map/while/body/slice | solution.py:69
  78.3 0.6 fusion.22
  79.0 0.6 fusion.23
  79.6 0.5 bitcast_reduce_fusion.2
  80.1 0.6 convert_reduce_fusion.2
  80.7 0.8 fusion.24
  81.6 0.2 copy.47
  81.8 0.1 select_convert_fusion
  81.9 0.4 copy.48
  82.3 0.5 broadcast.29
  82.8 2.2 %reduce = bf16[512,256]{1,0:T(8,128)(2,1)S(1)} reduce(bf16[512,1,256]{2,1,0:T(2,128)(2,1)S(1)} %bitcast.60, bf16[]{:T(256)} %broadcast.29), dimensions={1}, to_apply=%bitcast.37.reduce_sub_computation | reduce | bytes 524290
  85.0 0.1 reshape.30
  85.1 12.3 %all_to_all.34 = bf16[8,2,8192]{2,1,0:T(2,128)(2,1)S(1)} all-to-all(bf16[8,2,8192]{2,1,0:T(2,128)(2,1)S(1)} %reshape.30), channel_id=1, replica_groups=mesh['span'=4,'seq'=8] {'seq'}, dimensions={0} | all-to-all | bytes 524288 | tf_op jit(solution)/shard_map/all_to_all | solution.py:77
  97.4 0.3 reshape.31
  97.7 0.7 copy.56
  (13 shorter events, 0.3 us)
Async XLA Ops:
  6.5 56.4 %all-gather.2.cloned.1.call-start = ((), (), s32[]{:S(2)}) async-start(), calls=%async_computation.2 | async-start | bytes 2621440 | tf_op jit(solution)/shard_map/all_gather | solution.py:60
  39.7 1.1 %copy-start = (s32[4]{0:T(128)S(1)}, s32[4]{0:T(128)}, u32[]{:S(2)}) copy-start(s32[4]{0:T(128)} %param.5) | copy-start | bytes 52
Sparse Core Ops, SparseCore 0:
  40.9 21.9 all-gather.1
where the time goes:
time: 106 us; the launch traced here: 105 us
  blocking collectives  37.1 us (35%)
  waiting for transfers between devices  20.7 us (20%)
  local copies, waits for them, and re-layouts  17.5 us (17%)
  between operations  13.6 us (13%)
  other arithmetic  11.2 us (11%)
  matrix products  5.12 us (5%)
    all_to_all x1, blocking collectives, shards(): spread = lax.all_to_all(qkv, 'seq', split_axis=3, concat_axis=2, tiled=True)  24.7 us
    all_gather x1, waiting for transfers between devices, shards(): arrived_block = lax.all_gather(pair_heads, 'span', axis=2, tiled=True)  20.7 us
    all_to_all x1, blocking collectives, shards(): lax.all_to_all(merged, 'seq', split_axis=1, concat_axis=2, tiled=True)  12.3 us
    unnamed x10, local copies, waits for them, and re-layouts  8.1 us
    slice x4, local copies, waits for them, and re-layouts, add_single(): block_part[1]  5.59 us
    dot_general x4, matrix products, block_terms(): jnp.einsum('hqk,hke->hqe', weights, values, preferred_element_type=jnp.fl...  3.26 us
    reduce_sum x4, other arithmetic, live_keys(): live_count = jnp.sum(jnp.where(span_list == other_index, lengths, 0))  2.56 us
    reduce_sum x4, other arithmetic, block_terms(): weight_sum = jnp.sum(weights.astype(jnp.float32), axis=-1)  2.56 us
  transfers between devices with their start and end apart: 1, of which 1 were waited for; matrix products, arithmetic and copies ran while one was open for 1% of the time, Pallas kernels for 0%

commit v1 on v0

v1 whole, which is shorter than its diff:
```python
import functools

import jax
import jax.numpy as jnp
from jax import lax
from jax.experimental import pallas as pl
from jax.experimental.pallas import tpu as pltpu
from jax.sharding import PartitionSpec as P

HD = 128
MASKED = -1e30
LOG2E = 1.4426950408889634
MESH = pl.DeviceIdType.MESH


def kernel(
    spans, ranks, heads, rows, lengths_ref, qkv_ref, out_ref,
    keys, queries, results,
    pair_send, query_send, result_send, forward_send,
    pair_recv, query_recv, result_recv,
):
    span = lax.axis_index("span")
    me = lax.axis_index("seq")
    tokens = rows * ranks
    query_tile = min(256, tokens)

    barrier = pltpu.get_barrier_semaphore()

    def greet(k, carry):
        pl.semaphore_signal(
            barrier, inc=1, device_id=(span, lax.rem(me + k, ranks)), device_id_type=MESH
        )
        return carry

    lax.fori_loop(1, ranks, greet, 0)

    @pl.when(span > 0)
    def _():
        pl.semaphore_signal(barrier, inc=1, device_id=(span - 1, me), device_id_type=MESH)

    @pl.when(span < spans - 1)
    def _():
        pl.semaphore_signal(barrier, inc=1, device_id=(span + 1, me), device_id_type=MESH)

    def block_rows(rank):
        return pl.ds(pl.multiple_of(rank * rows, rows), rows)

    def columns(rank, h):
        return pl.ds(pl.multiple_of((rank * heads + h) * HD, HD), HD)

    def pair_slot(h, rank, j):
        return keys.at[h, :, j, block_rows(rank), :]

    def query_slot(h, rank):
        return queries.at[h, block_rows(rank), :]

    def offset(i):
        half = (i + 1) // 2
        return ranks // 2 + half - 2 * half * lax.rem(i, 2)

    def pair_source(rank, h):
        return qkv_ref.at[pl.ds(1, 2), 0, :, columns(rank, h)]

    def query_source(rank, h):
        return qkv_ref.at[0, 0, :, columns(rank, h)]

    def own_pair(h):
        return pltpu.make_async_copy(
            pair_source(me, h), pair_slot(h, me, span), pair_recv.at[h, me, span]
        )

    def own_query(h):
        return pltpu.make_async_copy(
            query_source(me, h), query_slot(h, me), query_recv.at[h, me]
        )

    def send_pair(h, rank):
        return pltpu.make_async_remote_copy(
            src_ref=pair_source(rank, h),
            dst_ref=pair_slot(h, me, span),
            send_sem=pair_send.at[h, rank],
            recv_sem=pair_recv.at[h, me, span],
            device_id=(span, rank),
            device_id_type=MESH,
        )

    def send_query(h, rank):
        return pltpu.make_async_remote_copy(
            src_ref=query_source(rank, h),
            dst_ref=query_slot(h, me),
            send_sem=query_send.at[h, rank],
            recv_sem=query_recv.at[h, me],
            device_id=(span, rank),
            device_id_type=MESH,
        )

    def send_result(h, rank):
        return pltpu.make_async_remote_copy(
            src_ref=results.at[h, block_rows(rank), :],
            dst_ref=out_ref.at[0, :, columns(me, h)],
            send_sem=result_send.at[h, rank],
            recv_sem=result_recv.at[h, me],
            device_id=(span, rank),
            device_id_type=MESH,
        )

    def forward(h, rank, j):
        return pltpu.make_async_remote_copy(
            src_ref=pair_slot(h, rank, j),
            dst_ref=pair_slot(h, rank, j),
            send_sem=forward_send.at[h, rank, j],
            recv_sem=pair_recv.at[h, rank, j],
            device_id=(span + 1, me),
            device_id_type=MESH,
        )

    def wait_bytes(ref, sem):
        pltpu.make_async_copy(ref, ref, sem).wait()

    for h in range(heads):
        own_pair(h).start()
        own_query(h).start()

    pl.semaphore_wait(
        barrier,
        ranks - 1 + (span > 0).astype(jnp.int32) + (span < spans - 1).astype(jnp.int32),
    )

    for h in range(heads):

        def start_pair(i, carry, h=h):
            send_pair(h, lax.rem(me + offset(i), ranks)).start()
            return carry

        def start_query(i, carry, h=h):
            send_query(h, lax.rem(me + offset(i), ranks)).start()
            return carry

        lax.fori_loop(0, ranks - 1, start_pair, 0)
        lax.fori_loop(0, ranks - 1, start_query, 0)

    def pass_on(h):
        def one_rank(rank):
            def one_span(i, carry):
                j = span - i
                wait_bytes(pair_slot(h, rank, j), pair_recv.at[h, rank, j])

                @pl.when(span < spans - 1)
                def _():
                    forward(h, rank, j).start()

                return carry

            lax.fori_loop(0, span + 1, one_span, 0)

        one_rank(me)

        def step(i, carry):
            one_rank(lax.rem(me - offset(i) + ranks, ranks))
            return carry

        lax.fori_loop(0, ranks - 1, step, 0)

    def attend(h):
        def wait_query(rank, carry):
            wait_bytes(query_slot(h, rank), query_recv.at[h, rank])
            return carry

        lax.fori_loop(0, ranks, wait_query, 0)
        own_count = lengths_ref[span]

        def one_tile(tile, carry):
            first = pl.multiple_of(tile * query_tile, query_tile)
            q = queries[h, pl.ds(first, query_tile), :]

            def one_span(j, state):
                peak, total, acc = state
                k = keys[h, 0, j]
                v = keys[h, 1, j]
                scores = lax.dot_general(
                    q, k, (((1,), (1,)), ((), ())), preferred_element_type=jnp.float32
                )
                position = lax.broadcasted_iota(jnp.int32, scores.shape, 1)
                scores = jnp.where(position < lengths_ref[j], scores, MASKED)
                new_peak = jnp.maximum(peak, jnp.max(scores, axis=1, keepdims=True))
                weights = jnp.exp2((scores - new_peak) * (LOG2E * HD**-0.5)).astype(jnp.bfloat16)
                scale = jnp.exp2((peak - new_peak) * (LOG2E * HD**-0.5))
                total = total * scale + jnp.sum(
                    weights.astype(jnp.float32), axis=1, keepdims=True
                )
                acc = acc * scale + jnp.dot(weights, v, preferred_element_type=jnp.float32)
                return new_peak, total, acc

            peak, total, acc = lax.fori_loop(
                0,
                span + 1,
                one_span,
                (
                    jnp.full((query_tile, 1), MASKED, jnp.float32),
                    jnp.zeros((query_tile, 1), jnp.float32),
                    jnp.zeros((query_tile, HD), jnp.float32),
                ),
            )
            position = first + lax.broadcasted_iota(jnp.int32, acc.shape, 0)
            value = jnp.where(position < own_count, acc / total, 0.0)
            results[h, pl.ds(first, query_tile), :] = value.astype(jnp.bfloat16)

            def start_result(i, carry):
                rank = tile * (query_tile // rows) + i

                @pl.when(rank != me)
                def _():
                    send_result(h, rank).start()

                @pl.when(rank == me)
                def _():
                    pltpu.make_async_copy(
                        results.at[h, block_rows(me), :],
                        out_ref.at[0, :, columns(me, h)],
                        result_recv.at[h, me],
                    ).start()

                return carry

            lax.fori_loop(0, query_tile // rows, start_result, 0)
            return carry

        lax.fori_loop(0, tokens // query_tile, one_tile, 0)

    for h in range(heads):
        pass_on(h)
        attend(h)

    for h in range(heads):

        def finish(i, carry, h=h):
            rank = lax.rem(me + i, ranks)
            send_pair(h, rank).wait_send()
            send_query(h, rank).wait_send()
            send_result(h, rank).wait_send()
            return carry

        lax.fori_loop(1, ranks, finish, 0)

        @pl.when(span < spans - 1)
        def _(h=h):
            def finish_rank(rank, carry):
                def finish_span(j, carry):
                    forward(h, rank, j).wait_send()
                    return carry

                return lax.fori_loop(0, span + 1, finish_span, carry)

            lax.fori_loop(0, ranks, finish_rank, 0)

        def arrived(rank, carry, h=h):
            wait_bytes(out_ref.at[0, :, columns(rank, h)], result_recv.at[h, rank])
            return carry

        lax.fori_loop(0, ranks, arrived, 0)


def shards(spans, ranks, qkv, lengths):
    rows, features = qkv.shape[2], qkv.shape[3]
    heads = features // HD // ranks
    tokens = rows * ranks
    dma = pltpu.SemaphoreType.DMA
    return pl.pallas_call(
        functools.partial(kernel, spans, ranks, heads, rows),
        out_shape=jax.ShapeDtypeStruct((1, rows, features), jnp.bfloat16),
        in_specs=[
            pl.BlockSpec(memory_space=pltpu.SMEM),
            pl.BlockSpec(memory_space=pl.ANY),
        ],
        out_specs=pl.BlockSpec(memory_space=pl.ANY),
        scratch_shapes=[
            pltpu.VMEM((heads, 2, spans, tokens, HD), jnp.bfloat16),
            pltpu.VMEM((heads, tokens, HD), jnp.bfloat16),
            pltpu.VMEM((heads, tokens, HD), jnp.bfloat16),
            dma((heads, ranks)),
            dma((heads, ranks)),
            dma((heads, ranks)),
            dma((heads, ranks, spans)),
            dma((heads, ranks, spans)),
            dma((heads, ranks)),
            dma((heads, ranks)),
        ],
        compiler_params=pltpu.CompilerParams(
            collective_id=0, has_side_effects=True, vmem_limit_bytes=40 * 2**20
        ),
    )(lengths, qkv)


def solution(mesh):
    in_specs = (P(None, "span", "seq", None), P())
    out_specs = P("span", "seq", None)
    body = functools.partial(shards, mesh.shape["span"], mesh.shape["seq"])
    return jax.shard_map(body, mesh=mesh, in_specs=in_specs, out_specs=out_specs, check_vma=False)
```

time: 106 us -> 41.1 us (0.39)
  Pallas kernels: 0 us -> 38.3 us
  blocking collectives: 37.1 us -> 0 us
  waiting for transfers between devices: 20.7 us -> 0 us
  local copies, waits for them, and re-layouts: 17.5 us -> 2.49 us
  between operations: 13.6 us -> 0.01 us
  other arithmetic: 11.2 us -> 0 us
  matrix products: 5.12 us -> 0 us
    pallas_call x0 -> x1, Pallas kernels: none -> 38.3 us  [shards(): pl.pallas_call(functools.partial(kernel, spans, ranks, heads, rows), out_...]
    all_to_all x2 -> x0, blocking collectives: 37.1 us -> none  [the longest x1 24.7 us: shards(): spread = lax.all_to_all(qkv, 'seq', split_axis=3, concat_axis=2, tiled=True)]
    all_gather x1 -> x0, waiting for transfers between devices: 20.7 us -> none  [shards(): arrived_block = lax.all_gather(pair_heads, 'span', axis=2, tiled=True)]
    slice x8 -> x0, local copies, waits for them, and re-layouts: 5.8 us -> none  [the longest x4 5.59 us: add_single(): block_part[1]]
    reduce_sum x9 -> x0, other arithmetic: 5.74 us -> none  [the longest x4 2.56 us: live_keys(): live_count = jnp.sum(jnp.where(span_list == other_index, lengths, 0))]
    unnamed x10 -> x5, local copies, waits for them, and re-layouts: 8.1 us -> 2.49 us
    dot_general x8 -> x0, matrix products: 5.12 us -> none  [the longest x4 3.26 us: block_terms(): jnp.einsum('hqk,hke->hqe', weights, values, preferred_element_type=jnp.fl...]
    and x4 -> x0, other arithmetic: 2.48 us -> none  [live_keys(): return (other_index <= span_index) & (positions < live_count)]
  transfers between devices with their start and end apart: 1 -> 0, of which waited for: 1 -> 0; matrix products, arithmetic and copies ran while one was open for 1% -> 0% of each run, Pallas kernels for 0% -> 0%
where the time goes in v1:
time: 41.1 us; the launch traced here: 40.8 us
  Pallas kernels  38.3 us (93%)
  local copies, waits for them, and re-layouts  2.49 us (6%)
    pallas_call x1, Pallas kernels, shards(): pl.pallas_call(functools.partial(kernel, spans, ranks, heads, rows), out_...  38.3 us
    unnamed x5, local copies, waits for them, and re-layouts  2.49 us

profile of v1, /device:TPU:5, one launch (start us, length us, event | category | flops | bytes accessed | tf_op | source)
XLA Modules:
  0.0 40.8 jit_solution(15311463249247599042)
XLA Ops:
  0.0 0.0 copy-start
  0.0 1.1 %copy-done = bf16[3,1,64,2048]{3,2,1,0:T(8,128)(2,1)S(1)} copy-done((bf16[3,1,64,2048]{3,2,1,0:T(8,128)(2,1)S(1)}, bf16[3,1,64,2048]{3,2,1,0:T(8,128)(2,1)}, u32[]{:S(2)}) %copy-start) | copy-done | bytes 786456
  1.1 0.0 copy-start.1
  1.1 0.7 %copy-done.1 = s32[4]{0:T(128)S(1)} copy-done((s32[4]{0:T(128)S(1)}, s32[4]{0:T(128)}, u32[]{:S(2)}) %copy-start.1) | copy-done | bytes 40
  1.8 38.3 %shard_map.28 = bf16[1,64,2048]{2,1,0:T(8,128)(2,1)S(1)} custom-call(s32[4]{0:T(128)S(1)} %copy-done.1, bf16[3,1,64,2048]{3,2,1,0:T(8,128)(2,1)S(1)} %copy-done), custom_call_target="tpu_custom_call" | custom-call | tf_op jit(solution)/shard_map/pallas_call | solution.py:268
  40.1 0.7 %copy.4 = bf16[1,64,2048]{2,1,0:T(8,128)(2,1)} copy(bf16[1,64,2048]{2,1,0:T(8,128)(2,1)S(1)} %shard_map.28) | data formatting | bytes 524288
Async XLA Ops:
  0.0 1.1 %copy-start = (bf16[3,1,64,2048]{3,2,1,0:T(8,128)(2,1)S(1)}, bf16[3,1,64,2048]{3,2,1,0:T(8,128)(2,1)}, u32[]{:S(2)}) copy-start(bf16[3,1,64,2048]{3,2,1,0:T(8,128)(2,1)} %qkv_ref.1) | copy-start | bytes 2359300
  1.1 0.7 %copy-start.1 = (s32[4]{0:T(128)S(1)}, s32[4]{0:T(128)}, u32[]{:S(2)}) copy-start(s32[4]{0:T(128)} %lengths_ref.1) | copy-start | bytes 52

commit v2 on v1

--- a/solution.py
+++ b/solution.py
@@ -14,8 +14,8 @@
 
 
 def kernel(
-    spans, ranks, heads, rows, lengths_ref, qkv_ref, out_ref,
-    keys, queries, results,
+    spans, ranks, heads, rows, lengths_hbm, qkv_ref, out_ref,
+    keys, queries, results, peaks, totals, sums, lengths_ref, lengths_sem,
     pair_send, query_send, result_send, forward_send,
     pair_recv, query_recv, result_recv,
 ):
@@ -23,6 +23,7 @@
     me = lax.axis_index("seq")
     tokens = rows * ranks
     query_tile = min(256, tokens)
+    half = ranks // 2
 
     barrier = pltpu.get_barrier_semaphore()
 
@@ -54,9 +55,16 @@
     def query_slot(h, rank):
         return queries.at[h, block_rows(rank), :]
 
-    def offset(i):
-        half = (i + 1) // 2
-        return ranks // 2 + half - 2 * half * lax.rem(i, 2)
+    def partner(k):
+        total = 0
+        for bit in range(ranks.bit_length() - 1):
+            unit = 2**bit
+            total += lax.rem(me // unit + k // unit, 2) * unit
+        return total
+
+    def send_step(i):
+        odd = lax.rem(i, 2)
+        return odd * ((i + 1) // 2) + (1 - odd) * (half + i // 2)
 
     def pair_source(rank, h):
         return qkv_ref.at[pl.ds(1, 2), 0, :, columns(rank, h)]
@@ -117,6 +125,8 @@
     def wait_bytes(ref, sem):
         pltpu.make_async_copy(ref, ref, sem).wait()
 
+    read_lengths = pltpu.make_async_copy(lengths_hbm, lengths_ref, lengths_sem)
+    read_lengths.start()
     for h in range(heads):
         own_pair(h).start()
         own_query(h).start()
@@ -129,81 +139,94 @@
     for h in range(heads):
 
         def start_pair(i, carry, h=h):
-            send_pair(h, lax.rem(me + offset(i), ranks)).start()
+            send_pair(h, partner(send_step(i))).start()
             return carry
 
         def start_query(i, carry, h=h):
-            send_query(h, lax.rem(me + offset(i), ranks)).start()
+            send_query(h, partner(send_step(i))).start()
             return carry
 
         lax.fori_loop(0, ranks - 1, start_pair, 0)
         lax.fori_loop(0, ranks - 1, start_query, 0)
 
-    def pass_on(h):
-        def one_rank(rank):
-            def one_span(i, carry):
-                j = span - i
-                wait_bytes(pair_slot(h, rank, j), pair_recv.at[h, rank, j])
-
-                @pl.when(span < spans - 1)
-                def _():
-                    forward(h, rank, j).start()
-
-                return carry
-
-            lax.fori_loop(0, span + 1, one_span, 0)
-
-        one_rank(me)
-
+    def pass_on(h, j, first, last):
+        def step(k, carry):
+            rank = partner(k)
+            wait_bytes(pair_slot(h, rank, j), pair_recv.at[h, rank, j])
+
+            @pl.when(span < spans - 1)
+            def _():
+                forward(h, rank, j).start()
+
+            return carry
+
+        lax.fori_loop(first, last, step, 0)
+
+    def pass_near(h):
         def step(i, carry):
-            one_rank(lax.rem(me - offset(i) + ranks, ranks))
-            return carry
-
-        lax.fori_loop(0, ranks - 1, step, 0)
-
-    def attend(h):
-        def wait_query(rank, carry):
+            pass_on(h, span - i, 0, half)
+            return carry
+
+        lax.fori_loop(0, span + 1, step, 0)
+
+    def pass_far(h, j):
+        pass_on(h, j, half, ranks)
+
+    def wait_queries(h):
+        def step(rank, carry):
             wait_bytes(query_slot(h, rank), query_recv.at[h, rank])
             return carry
 
-        lax.fori_loop(0, ranks, wait_query, 0)
-        own_count = lengths_ref[span]
-
+        lax.fori_loop(0, ranks, step, 0)
+
+    def add_block(h, j, here, live):
+        scores = lax.dot_general(
+            queries[h, here, :],
+            keys[h, 0, j],
+            (((1,), (1,)), ((), ())),
+            preferred_element_type=jnp.float32,
+        )
+        position = lax.broadcasted_iota(jnp.int32, scores.shape, 1)
+        scores = jnp.where(position < live, scores, MASKED)
+        peak = peaks[here, :]
+        new_peak = jnp.maximum(peak, jnp.max(scores, axis=1, keepdims=True))
+        weights = jnp.exp2((scores - new_peak) * (LOG2E * HD**-0.5)).astype(jnp.bfloat16)
+        scale = jnp.exp2((peak - new_peak) * (LOG2E * HD**-0.5))
+        total = totals[here, :] * scale + jnp.sum(
+            weights.astype(jnp.float32), axis=1, keepdims=True
+        )
+        acc = sums[here, :] * scale + jnp.dot(
+            weights, keys[h, 1, j], preferred_element_type=jnp.float32
+        )
+        return new_peak, total, acc
+
+    def tile_rows(tile):
+        return pl.ds(pl.multiple_of(tile * query_tile, query_tile), query_tile)
+
+    tiles = tokens // query_tile
+
+    def start_state():
+        peaks[...] = jnp.full(peaks.shape, MASKED, jnp.float32)
+        totals[...] = jnp.zeros(totals.shape, jnp.float32)
+        sums[...] = jnp.zeros(sums.shape, jnp.float32)
+
+    def middle_block(h, j):
         def one_tile(tile, carry):
-            first = pl.multiple_of(tile * query_tile, query_tile)
-            q = queries[h, pl.ds(first, query_tile), :]
-
-            def one_span(j, state):
-                peak, total, acc = state
-                k = keys[h, 0, j]
-                v = keys[h, 1, j]
-                scores = lax.dot_general(
-                    q, k, (((1,), (1,)), ((), ())), preferred_element_type=jnp.float32
-                )
-                position = lax.broadcasted_iota(jnp.int32, scores.shape, 1)
-                scores = jnp.where(position < lengths_ref[j], scores, MASKED)
-                new_peak = jnp.maximum(peak, jnp.max(scores, axis=1, keepdims=True))
-                weights = jnp.exp2((scores - new_peak) * (LOG2E * HD**-0.5)).astype(jnp.bfloat16)
-                scale = jnp.exp2((peak - new_peak) * (LOG2E * HD**-0.5))
-                total = total * scale + jnp.sum(
-                    weights.astype(jnp.float32), axis=1, keepdims=True
-                )
-                acc = acc * scale + jnp.dot(weights, v, preferred_element_type=jnp.float32)
-                return new_peak, total, acc
-
-            peak, total, acc = lax.fori_loop(
-                0,
-                span + 1,
-                one_span,
-                (
-                    jnp.full((query_tile, 1), MASKED, jnp.float32),
-                    jnp.zeros((query_tile, 1), jnp.float32),
-                    jnp.zeros((query_tile, HD), jnp.float32),
-                ),
+            here = tile_rows(tile)
+            peaks[here, :], totals[here, :], sums[here, :] = add_block(
+                h, j, here, lengths_ref[j]
             )
-            position = first + lax.broadcasted_iota(jnp.int32, acc.shape, 0)
-            value = jnp.where(position < own_count, acc / total, 0.0)
-            results[h, pl.ds(first, query_tile), :] = value.astype(jnp.bfloat16)
+            return carry
+
+        lax.fori_loop(0, tiles, one_tile, 0)
+
+    def last_block(h):
+        def one_tile(tile, carry):
+            here = tile_rows(tile)
+            _, total, acc = add_block(h, 0, here, lengths_ref[0])
+            position = tile * query_tile + lax.broadcasted_iota(jnp.int32, acc.shape, 0)
+            value = jnp.where(position < lengths_ref[span], acc / total, 0.0)
+            results[h, here, :] = value.astype(jnp.bfloat16)
 
             def start_result(i, carry):
                 rank = tile * (query_tile // rows) + i
@@ -225,11 +248,32 @@
             lax.fori_loop(0, query_tile // rows, start_result, 0)
             return carry
 
-        lax.fori_loop(0, tokens // query_tile, one_tile, 0)
-
-    for h in range(heads):
-        pass_on(h)
-        attend(h)
+        lax.fori_loop(0, tiles, one_tile, 0)
+
+    read_lengths.wait()
+    for h in range(heads):
+        pass_near(h)
+    for h in range(heads):
+        start_state()
+        pass_far(h, span)
+
+        @pl.when(span > 0)
+        def _(h=h):
+            pass_far(h, span - 1)
+
+        wait_queries(h)
+
+        def step(i, carry, h=h):
+            middle_block(h, span - i)
+
+            @pl.when(i + 1 < span)
+            def _():
+                pass_far(h, span - i - 2)
+
+            return carry
+
+        lax.fori_loop(0, span, step, 0)
+        last_block(h)
 
     for h in range(heads):
 
@@ -269,14 +313,19 @@
         functools.partial(kernel, spans, ranks, heads, rows),
         out_shape=jax.ShapeDtypeStruct((1, rows, features), jnp.bfloat16),
         in_specs=[
-            pl.BlockSpec(memory_space=pltpu.SMEM),
-            pl.BlockSpec(memory_space=pl.ANY),
+            pl.BlockSpec(memory_space=pltpu.HBM),
+            pl.BlockSpec(memory_space=pltpu.HBM),
         ],
         out_specs=pl.BlockSpec(memory_space=pl.ANY),
         scratch_shapes=[
             pltpu.VMEM((heads, 2, spans, tokens, HD), jnp.bfloat16),
             pltpu.VMEM((heads, tokens, HD), jnp.bfloat16),
             pltpu.VMEM((heads, tokens, HD), jnp.bfloat16),
+            pltpu.VMEM((tokens, 1), jnp.float32),
+            pltpu.VMEM((tokens, 1), jnp.float32),
+            pltpu.VMEM((tokens, HD), jnp.float32),
+            pltpu.SMEM((spans,), jnp.int32),
+            dma(()),
             dma((heads, ranks)),
             dma((heads, ranks)),
             dma((heads, ranks)),

time: 41.1 us -> 38.6 us (0.939)
  Pallas kernels: 38.3 us -> 35.9 us
    pallas_call x1, Pallas kernels: 38.3 us -> 35.9 us  [shards(): pl.pallas_call(functools.partial(kernel, spans, ranks, heads, rows), out_...]
where the time goes in v2:
time: 38.6 us; the launch traced here: 38.4 us
  Pallas kernels  35.9 us (93%)
  local copies, waits for them, and re-layouts  2.49 us (6%)
    pallas_call x1, Pallas kernels, shards(): pl.pallas_call(functools.partial(kernel, spans, ranks, heads, rows), out_...  35.9 us
    unnamed x5, local copies, waits for them, and re-layouts  2.49 us

profile of v2, /device:TPU:5, one launch (start us, length us, event | category | flops | bytes accessed | tf_op | source)
XLA Modules:
  0.0 38.4 jit_solution(12692417898297835381)
XLA Ops:
  0.0 0.0 copy-start
  0.0 1.1 %copy-done = bf16[3,1,64,2048]{3,2,1,0:T(8,128)(2,1)S(1)} copy-done((bf16[3,1,64,2048]{3,2,1,0:T(8,128)(2,1)S(1)}, bf16[3,1,64,2048]{3,2,1,0:T(8,128)(2,1)}, u32[]{:S(2)}) %copy-start) | copy-done | bytes 786456
  1.1 0.0 copy-start.1
  1.1 0.7 %copy-done.1 = s32[4]{0:T(128)S(1)} copy-done((s32[4]{0:T(128)S(1)}, s32[4]{0:T(128)}, u32[]{:S(2)}) %copy-start.1) | copy-done | bytes 40
  1.8 35.9 %shard_map.28 = bf16[1,64,2048]{2,1,0:T(8,128)(2,1)S(1)} custom-call(s32[4]{0:T(128)S(1)} %copy-done.1, bf16[3,1,64,2048]{3,2,1,0:T(8,128)(2,1)S(1)} %copy-done), custom_call_target="tpu_custom_call" | custom-call | tf_op jit(solution)/shard_map/pallas_call | solution.py:312
  37.7 0.7 %copy.4 = bf16[1,64,2048]{2,1,0:T(8,128)(2,1)} copy(bf16[1,64,2048]{2,1,0:T(8,128)(2,1)S(1)} %shard_map.28) | data formatting | bytes 524288
Async XLA Ops:
  0.0 1.1 %copy-start = (bf16[3,1,64,2048]{3,2,1,0:T(8,128)(2,1)S(1)}, bf16[3,1,64,2048]{3,2,1,0:T(8,128)(2,1)}, u32[]{:S(2)}) copy-start(bf16[3,1,64,2048]{3,2,1,0:T(8,128)(2,1)} %qkv_ref.1) | copy-start | bytes 2359300
  1.1 0.7 %copy-start.1 = (s32[4]{0:T(128)S(1)}, s32[4]{0:T(128)}, u32[]{:S(2)}) copy-start(s32[4]{0:T(128)} %lengths_hbm.1) | copy-start | bytes 52

commit v3 on v2

--- a/solution.py
+++ b/solution.py
@@ -136,18 +136,32 @@
         ranks - 1 + (span > 0).astype(jnp.int32) + (span < spans - 1).astype(jnp.int32),
     )
 
-    for h in range(heads):
-
-        def start_pair(i, carry, h=h):
-            send_pair(h, partner(send_step(i))).start()
-            return carry
-
-        def start_query(i, carry, h=h):
-            send_query(h, partner(send_step(i))).start()
-            return carry
-
-        lax.fori_loop(0, ranks - 1, start_pair, 0)
-        lax.fori_loop(0, ranks - 1, start_query, 0)
+    groups = [(h, make) for h in range(heads) for make in (send_pair, send_query)]
+    in_flight = []
+
+    def start_group(h, make):
+        def step(i, carry):
+            make(h, partner(send_step(i))).start()
+            return carry
+
+        lax.fori_loop(0, ranks - 1, step, 0)
+
+    def drain_group(h, make):
+        def step(i, carry):
+            make(h, partner(send_step(i))).wait_send()
+            return carry
+
+        lax.fori_loop(0, ranks - 1, step, 0)
+
+    def advance():
+        if groups:
+            if len(in_flight) == 2:
+                drain_group(*in_flight.pop(0))
+            in_flight.append(groups.pop(0))
+            start_group(*in_flight[-1])
+
+    advance()
+    advance()
 
     def pass_on(h, j, first, last):
         def step(k, carry):
@@ -163,11 +177,14 @@
         lax.fori_loop(first, last, step, 0)
 
     def pass_near(h):
+        pass_on(h, span, 0, half)
+        advance()
+
         def step(i, carry):
             pass_on(h, span - i, 0, half)
             return carry
 
-        lax.fori_loop(0, span + 1, step, 0)
+        lax.fori_loop(1, span + 1, step, 0)
 
     def pass_far(h, j):
         pass_on(h, j, half, ranks)
@@ -251,11 +268,11 @@
         lax.fori_loop(0, tiles, one_tile, 0)
 
     read_lengths.wait()
-    for h in range(heads):
-        pass_near(h)
+    pass_near(0)
     for h in range(heads):
         start_state()
         pass_far(h, span)
+        advance()
 
         @pl.when(span > 0)
         def _(h=h):
@@ -273,14 +290,17 @@
             return carry
 
         lax.fori_loop(0, span, step, 0)
+        if h + 1 < heads:
+            pass_near(h + 1)
         last_block(h)
+
+    for group in in_flight:
+        drain_group(*group)
 
     for h in range(heads):
 
         def finish(i, carry, h=h):
             rank = lax.rem(me + i, ranks)
-            send_pair(h, rank).wait_send()
-            send_query(h, rank).wait_send()
             send_result(h, rank).wait_send()
             return carry
 
@@ -335,7 +355,7 @@
             dma((heads, ranks)),
         ],
         compiler_params=pltpu.CompilerParams(
-            collective_id=0, has_side_effects=True, vmem_limit_bytes=40 * 2**20
+            collective_id=0, has_side_effects=True, vmem_limit_bytes=64 * 2**20
         ),
     )(lengths, qkv)
 

time: 38.6 us -> 37.8 us (0.979)
  local copies, waits for them, and re-layouts: 2.49 us -> 1.67 us
    unnamed x5 -> x1, local copies, waits for them, and re-layouts: 2.49 us -> 1.67 us
where the time goes in v3:
time: 37.8 us; the launch traced here: 37.6 us
  Pallas kernels  36 us (95%)
  local copies, waits for them, and re-layouts  1.67 us (4%)
    pallas_call x1, Pallas kernels, shards(): pl.pallas_call(functools.partial(kernel, spans, ranks, heads, rows), out_...  36 us
    unnamed x1, local copies, waits for them, and re-layouts  1.67 us

profile of v3, /device:TPU:5, one launch (start us, length us, event | category | flops | bytes accessed | tf_op | source)
XLA Modules:
  0.0 37.6 jit_solution(7034486853143061756)
XLA Ops:
  0.0 36.0 %shard_map.28 = bf16[1,64,2048]{2,1,0:T(8,128)(2,1)} custom-call(s32[4]{0:T(128)} %lengths_hbm.1, bf16[3,1,64,2048]{3,2,1,0:T(8,128)(2,1)} %qkv_ref.1), custom_call_target="tpu_custom_call" | custom-call | tf_op jit(solution)/shard_map/pallas_call | solution.py:332
  36.0 1.7 %copy.4 = bf16[1,64,2048]{2,1,0:T(8,128)(2,1)} copy(bf16[1,64,2048]{2,1,0:T(8,128)(2,1)} %shard_map.28) | data formatting | bytes 524288

commit v4 on v3

--- a/solution.py
+++ b/solution.py
@@ -15,7 +15,7 @@
 
 def kernel(
     spans, ranks, heads, rows, lengths_hbm, qkv_ref, out_ref,
-    keys, queries, results, peaks, totals, sums, lengths_ref, lengths_sem,
+    keys, queries, results, peaks, sums, lengths_ref, lengths_sem,
     pair_send, query_send, result_send, forward_send,
     pair_recv, query_recv, result_recv,
 ):
@@ -177,14 +177,11 @@
         lax.fori_loop(first, last, step, 0)
 
     def pass_near(h):
-        pass_on(h, span, 0, half)
-        advance()
-
         def step(i, carry):
             pass_on(h, span - i, 0, half)
             return carry
 
-        lax.fori_loop(1, span + 1, step, 0)
+        lax.fori_loop(0, span + 1, step, 0)
 
     def pass_far(h, j):
         pass_on(h, j, half, ranks)
@@ -196,57 +193,71 @@
 
         lax.fori_loop(0, ranks, step, 0)
 
-    def add_block(h, j, here, live):
-        scores = lax.dot_general(
-            queries[h, here, :],
-            keys[h, 0, j],
-            (((1,), (1,)), ((), ())),
-            preferred_element_type=jnp.float32,
-        )
-        position = lax.broadcasted_iota(jnp.int32, scores.shape, 1)
-        scores = jnp.where(position < live, scores, MASKED)
-        peak = peaks[here, :]
-        new_peak = jnp.maximum(peak, jnp.max(scores, axis=1, keepdims=True))
-        weights = jnp.exp2((scores - new_peak) * (LOG2E * HD**-0.5)).astype(jnp.bfloat16)
-        scale = jnp.exp2((peak - new_peak) * (LOG2E * HD**-0.5))
-        total = totals[here, :] * scale + jnp.sum(
-            weights.astype(jnp.float32), axis=1, keepdims=True
-        )
-        acc = sums[here, :] * scale + jnp.dot(
-            weights, keys[h, 1, j], preferred_element_type=jnp.float32
-        )
-        return new_peak, total, acc
-
-    def tile_rows(tile):
-        return pl.ds(pl.multiple_of(tile * query_tile, query_tile), query_tile)
-
     tiles = tokens // query_tile
+    side = min(2, tiles)
+    ones = jnp.ones((tokens, HD), jnp.bfloat16)
+
+    def add_block(h, j, first):
+        live = lax.broadcasted_iota(jnp.int32, (1, tokens), 1) < lengths_ref[j]
+        limit = jnp.where(live, -2 * MASKED, MASKED)
+        k = keys[h, 0, j]
+        v = jnp.concatenate([keys[h, 1, j], ones], axis=1)
+        states = []
+        for t in range(side):
+            here = pl.ds(first + t * query_tile, query_tile)
+            scores = lax.dot_general(
+                queries[h, here, :],
+                k,
+                (((1,), (1,)), ((), ())),
+                preferred_element_type=jnp.float32,
+            )
+            scores = jnp.minimum(scores, limit)
+            peak = peaks[here, :]
+            new_peak = jnp.maximum(peak, jnp.max(scores, axis=1, keepdims=True))
+            weights = jnp.exp2((scores - new_peak) * (LOG2E * HD**-0.5)).astype(jnp.bfloat16)
+            scale = jnp.exp2((peak - new_peak) * (LOG2E * HD**-0.5))
+            acc = sums[here, :] * scale + jnp.dot(
+                weights, v, preferred_element_type=jnp.float32
+            )
+            states.append((here, new_peak, acc))
+        return states
 
     def start_state():
         peaks[...] = jnp.full(peaks.shape, MASKED, jnp.float32)
-        totals[...] = jnp.zeros(totals.shape, jnp.float32)
         sums[...] = jnp.zeros(sums.shape, jnp.float32)
 
+    def each_group(body):
+        if tiles == side:
+            body(0)
+        else:
+
+            def step(group, carry):
+                body(pl.multiple_of(group * side * query_tile, side * query_tile))
+                return carry
+
+            lax.fori_loop(0, tiles // side, step, 0)
+
     def middle_block(h, j):
-        def one_tile(tile, carry):
-            here = tile_rows(tile)
-            peaks[here, :], totals[here, :], sums[here, :] = add_block(
-                h, j, here, lengths_ref[j]
-            )
-            return carry
-
-        lax.fori_loop(0, tiles, one_tile, 0)
+        def body(first):
+            for here, peak, acc in add_block(h, j, first):
+                peaks[here, :] = peak
+                sums[here, :] = acc
+
+        each_group(body)
 
     def last_block(h):
-        def one_tile(tile, carry):
-            here = tile_rows(tile)
-            _, total, acc = add_block(h, 0, here, lengths_ref[0])
-            position = tile * query_tile + lax.broadcasted_iota(jnp.int32, acc.shape, 0)
-            value = jnp.where(position < lengths_ref[span], acc / total, 0.0)
-            results[h, here, :] = value.astype(jnp.bfloat16)
+        def body(first):
+            for t, (here, _, acc) in enumerate(add_block(h, 0, first)):
+                position = (
+                    first + t * query_tile + lax.broadcasted_iota(jnp.int32, (query_tile, HD), 0)
+                )
+                value = jnp.where(
+                    position < lengths_ref[span], acc[:, :HD] / acc[:, HD:], 0.0
+                )
+                results[h, here, :] = value.astype(jnp.bfloat16)
 
             def start_result(i, carry):
-                rank = tile * (query_tile // rows) + i
+                rank = first // rows + i
 
                 @pl.when(rank != me)
                 def _():
@@ -262,22 +273,28 @@
 
                 return carry
 
-            lax.fori_loop(0, query_tile // rows, start_result, 0)
-            return carry
-
-        lax.fori_loop(0, tiles, one_tile, 0)
+            lax.fori_loop(0, side * query_tile // rows, start_result, 0)
+
+        each_group(body)
 
     read_lengths.wait()
     pass_near(0)
+    advance()
     for h in range(heads):
-        start_state()
         pass_far(h, span)
-        advance()
 
         @pl.when(span > 0)
         def _(h=h):
             pass_far(h, span - 1)
 
+        advance()
+        if h + 1 < heads:
+
+            @pl.when(span < spans - 1)
+            def _(h=h):
+                pass_near(h + 1)
+
+        start_state()
         wait_queries(h)
 
         def step(i, carry, h=h):
@@ -290,9 +307,12 @@
             return carry
 
         lax.fori_loop(0, span, step, 0)
+        last_block(h)
         if h + 1 < heads:
-            pass_near(h + 1)
-        last_block(h)
+
+            @pl.when(span == spans - 1)
+            def _(h=h):
+                pass_near(h + 1)
 
     for group in in_flight:
         drain_group(*group)
@@ -342,8 +362,7 @@
             pltpu.VMEM((heads, tokens, HD), jnp.bfloat16),
             pltpu.VMEM((heads, tokens, HD), jnp.bfloat16),
             pltpu.VMEM((tokens, 1), jnp.float32),
-            pltpu.VMEM((tokens, 1), jnp.float32),
-            pltpu.VMEM((tokens, HD), jnp.float32),
+            pltpu.VMEM((tokens, 2 * HD), jnp.float32),
             pltpu.SMEM((spans,), jnp.int32),
             dma(()),
             dma((heads, ranks)),

time: 37.8 us -> 38.7 us (1.024)
  Pallas kernels: 36 us -> 36.8 us
    pallas_call x1, Pallas kernels: 36 us -> 36.8 us  [shards(): pl.pallas_call(functools.partial(kernel, spans, ranks, heads, rows), out_...]
where the time goes in v4:
time: 38.7 us; the launch traced here: 38.5 us
  Pallas kernels  36.8 us (95%)
  local copies, waits for them, and re-layouts  1.67 us (4%)
    pallas_call x1, Pallas kernels, shards(): pl.pallas_call(functools.partial(kernel, spans, ranks, heads, rows), out_...  36.8 us
    unnamed x1, local copies, waits for them, and re-layouts  1.67 us

profile of v4, /device:TPU:5, one launch (start us, length us, event | category | flops | bytes accessed | tf_op | source)
XLA Modules:
  0.0 38.5 jit_solution(12131464903966735987)
XLA Ops:
  0.0 36.8 %shard_map.28 = bf16[1,64,2048]{2,1,0:T(8,128)(2,1)} custom-call(s32[4]{0:T(128)} %lengths_hbm.1, bf16[3,1,64,2048]{3,2,1,0:T(8,128)(2,1)} %qkv_ref.1), custom_call_target="tpu_custom_call" | custom-call | tf_op jit(solution)/shard_map/pallas_call | solution.py:352
  36.8 1.7 %copy.4 = bf16[1,64,2048]{2,1,0:T(8,128)(2,1)} copy(bf16[1,64,2048]{2,1,0:T(8,128)(2,1)} %shard_map.28) | data formatting | bytes 524288

commit v5 on v3

--- a/solution.py
+++ b/solution.py
@@ -15,15 +15,15 @@
 
 def kernel(
     spans, ranks, heads, rows, lengths_hbm, qkv_ref, out_ref,
-    keys, queries, results, peaks, totals, sums, lengths_ref, lengths_sem,
+    keys, queries, results,  lengths_ref, lengths_sem,
     pair_send, query_send, result_send, forward_send,
     pair_recv, query_recv, result_recv,
 ):
     span = lax.axis_index("span")
     me = lax.axis_index("seq")
     tokens = rows * ranks
-    query_tile = min(256, tokens)
     half = ranks // 2
+    query_tile = min(256, half * rows)
 
     barrier = pltpu.get_barrier_semaphore()
 
@@ -136,7 +136,7 @@
         ranks - 1 + (span > 0).astype(jnp.int32) + (span < spans - 1).astype(jnp.int32),
     )
 
-    groups = [(h, make) for h in range(heads) for make in (send_pair, send_query)]
+    groups = [(h, make) for make in (send_pair, send_query) for h in range(heads)]
     in_flight = []
 
     def start_group(h, make):
@@ -177,76 +177,60 @@
         lax.fori_loop(first, last, step, 0)
 
     def pass_near(h):
-        pass_on(h, span, 0, half)
-        advance()
-
         def step(i, carry):
             pass_on(h, span - i, 0, half)
             return carry
 
-        lax.fori_loop(1, span + 1, step, 0)
+        lax.fori_loop(0, span + 1, step, 0)
 
     def pass_far(h, j):
         pass_on(h, j, half, ranks)
 
-    def wait_queries(h):
-        def step(rank, carry):
+    ones = jnp.ones((tokens, HD), jnp.bfloat16)
+
+    def attend(h, first_rank):
+        def wait_query(i, carry):
+            rank = first_rank + i
             wait_bytes(query_slot(h, rank), query_recv.at[h, rank])
             return carry
 
-        lax.fori_loop(0, ranks, step, 0)
-
-    def add_block(h, j, here, live):
-        scores = lax.dot_general(
-            queries[h, here, :],
-            keys[h, 0, j],
-            (((1,), (1,)), ((), ())),
-            preferred_element_type=jnp.float32,
-        )
-        position = lax.broadcasted_iota(jnp.int32, scores.shape, 1)
-        scores = jnp.where(position < live, scores, MASKED)
-        peak = peaks[here, :]
-        new_peak = jnp.maximum(peak, jnp.max(scores, axis=1, keepdims=True))
-        weights = jnp.exp2((scores - new_peak) * (LOG2E * HD**-0.5)).astype(jnp.bfloat16)
-        scale = jnp.exp2((peak - new_peak) * (LOG2E * HD**-0.5))
-        total = totals[here, :] * scale + jnp.sum(
-            weights.astype(jnp.float32), axis=1, keepdims=True
-        )
-        acc = sums[here, :] * scale + jnp.dot(
-            weights, keys[h, 1, j], preferred_element_type=jnp.float32
-        )
-        return new_peak, total, acc
-
-    def tile_rows(tile):
-        return pl.ds(pl.multiple_of(tile * query_tile, query_tile), query_tile)
-
-    tiles = tokens // query_tile
-
-    def start_state():
-        peaks[...] = jnp.full(peaks.shape, MASKED, jnp.float32)
-        totals[...] = jnp.zeros(totals.shape, jnp.float32)
-        sums[...] = jnp.zeros(sums.shape, jnp.float32)
-
-    def middle_block(h, j):
+        lax.fori_loop(0, half, wait_query, 0)
+
         def one_tile(tile, carry):
-            here = tile_rows(tile)
-            peaks[here, :], totals[here, :], sums[here, :] = add_block(
-                h, j, here, lengths_ref[j]
+            first = pl.multiple_of(first_rank * rows + tile * query_tile, query_tile)
+            here = pl.ds(first, query_tile)
+            q = queries[h, here, :]
+
+            def add_block(j, state):
+                peak, acc = state
+                live = lax.broadcasted_iota(jnp.int32, (1, tokens), 1) < lengths_ref[j]
+                limit = jnp.where(live, -2 * MASKED, MASKED)
+                scores = lax.dot_general(
+                    q, keys[h, 0, j], (((1,), (1,)), ((), ())), preferred_element_type=jnp.float32
+                )
+                scores = jnp.minimum(scores, limit)
+                new_peak = jnp.maximum(peak, jnp.max(scores, axis=1, keepdims=True))
+                weights = jnp.exp2((scores - new_peak) * (LOG2E * HD**-0.5)).astype(jnp.bfloat16)
+                scale = jnp.exp2((peak - new_peak) * (LOG2E * HD**-0.5))
+                v = jnp.concatenate([keys[h, 1, j], ones], axis=1)
+                acc = acc * scale + jnp.dot(weights, v, preferred_element_type=jnp.float32)
+                return new_peak, acc
+
+            _, acc = lax.fori_loop(
+                0,
+                span + 1,
+                add_block,
+                (
+                    jnp.full((query_tile, 1), MASKED, jnp.float32),
+                    jnp.zeros((query_tile, 2 * HD), jnp.float32),
+                ),
             )
-            return carry
-
-        lax.fori_loop(0, tiles, one_tile, 0)
-
-    def last_block(h):
-        def one_tile(tile, carry):
-            here = tile_rows(tile)
-            _, total, acc = add_block(h, 0, here, lengths_ref[0])
-            position = tile * query_tile + lax.broadcasted_iota(jnp.int32, acc.shape, 0)
-            value = jnp.where(position < lengths_ref[span], acc / total, 0.0)
+            position = first + lax.broadcasted_iota(jnp.int32, (query_tile, HD), 0)
+            value = jnp.where(position < lengths_ref[span], acc[:, :HD] / acc[:, HD:], 0.0)
             results[h, here, :] = value.astype(jnp.bfloat16)
 
             def start_result(i, carry):
-                rank = tile * (query_tile // rows) + i
+                rank = first_rank + tile * (query_tile // rows) + i
 
                 @pl.when(rank != me)
                 def _():
@@ -265,34 +249,26 @@
             lax.fori_loop(0, query_tile // rows, start_result, 0)
             return carry
 
-        lax.fori_loop(0, tiles, one_tile, 0)
+        lax.fori_loop(0, half * rows // query_tile, one_tile, 0)
+
+    near = me // half * half
+    far = half - near
 
     read_lengths.wait()
-    pass_near(0)
-    for h in range(heads):
-        start_state()
-        pass_far(h, span)
+    for h in range(heads):
+        pass_near(h)
+    advance()
+    for h in range(heads):
+
+        def step(i, carry, h=h):
+            pass_far(h, span - i)
+            return carry
+
+        lax.fori_loop(0, span + 1, step, 0)
+        attend(h, near)
         advance()
-
-        @pl.when(span > 0)
-        def _(h=h):
-            pass_far(h, span - 1)
-
-        wait_queries(h)
-
-        def step(i, carry, h=h):
-            middle_block(h, span - i)
-
-            @pl.when(i + 1 < span)
-            def _():
-                pass_far(h, span - i - 2)
-
-            return carry
-
-        lax.fori_loop(0, span, step, 0)
-        if h + 1 < heads:
-            pass_near(h + 1)
-        last_block(h)
+    for h in range(heads):
+        attend(h, far)
 
     for group in in_flight:
         drain_group(*group)
@@ -329,7 +305,7 @@
     heads = features // HD // ranks
     tokens = rows * ranks
     dma = pltpu.SemaphoreType.DMA
-    return pl.pallas_call(
+    attended = pl.pallas_call(
         functools.partial(kernel, spans, ranks, heads, rows),
         out_shape=jax.ShapeDtypeStruct((1, rows, features), jnp.bfloat16),
         in_specs=[
@@ -341,9 +317,6 @@
             pltpu.VMEM((heads, 2, spans, tokens, HD), jnp.bfloat16),
             pltpu.VMEM((heads, tokens, HD), jnp.bfloat16),
             pltpu.VMEM((heads, tokens, HD), jnp.bfloat16),
-            pltpu.VMEM((tokens, 1), jnp.float32),
-            pltpu.VMEM((tokens, 1), jnp.float32),
-            pltpu.VMEM((tokens, HD), jnp.float32),
             pltpu.SMEM((spans,), jnp.int32),
             dma(()),
             dma((heads, ranks)),
@@ -358,6 +331,7 @@
             collective_id=0, has_side_effects=True, vmem_limit_bytes=64 * 2**20
         ),
     )(lengths, qkv)
+    return jnp.maximum(attended, jnp.finfo(jnp.bfloat16).min)
 
 
 def solution(mesh):

time: 37.8 us -> 43.3 us (1.15)
  Pallas kernels: 36 us -> 41.5 us
  other arithmetic: 0 us -> 1.68 us
  local copies, waits for them, and re-layouts: 1.67 us -> 0 us
    pallas_call x1, Pallas kernels: 36 us -> 41.5 us  [shards(): pl.pallas_call(functools.partial(kernel, spans, ranks, heads, rows), out_...]
    max x0 -> x1, other arithmetic: none -> 1.68 us  [shards(): return jnp.maximum(attended, jnp.finfo(jnp.bfloat16).min)]
    unnamed x1 -> x0, local copies, waits for them, and re-layouts: 1.67 us -> none
where the time goes in v5:
time: 43.3 us; the launch traced here: 43.1 us
  Pallas kernels  41.5 us (96%)
  other arithmetic  1.68 us (4%)
    pallas_call x1, Pallas kernels, shards(): pl.pallas_call(functools.partial(kernel, spans, ranks, heads, rows), out_...  41.5 us
    max x1, other arithmetic, shards(): return jnp.maximum(attended, jnp.finfo(jnp.bfloat16).min)  1.68 us

profile of v5, /device:TPU:5, one launch (start us, length us, event | category | flops | bytes accessed | tf_op | source)
XLA Modules:
  0.0 43.1 jit_solution(2702235497310867025)
XLA Ops:
  0.0 41.5 %shard_map.28 = bf16[1,64,2048]{2,1,0:T(8,128)(2,1)} custom-call(s32[4]{0:T(128)} %lengths_hbm.1, bf16[3,1,64,2048]{3,2,1,0:T(8,128)(2,1)} %qkv_ref.1), custom_call_target="tpu_custom_call" | custom-call | tf_op jit(solution)/shard_map/pallas_call | solution.py:308
  41.5 1.7 %broadcast_maximum_fusion = bf16[1,64,2048]{2,1,0:T(8,128)(2,1)} fusion(bf16[1,64,2048]{2,1,0:T(8,128)(2,1)} %shard_map.28), kind=kLoop, calls=%fused_computation | loop fusion | flops 131072 | bytes 524288 | tf_op jit(solution)/shard_map/max | solution.py:334

commit v6 on v3

--- a/solution.py
+++ b/solution.py
@@ -136,9 +136,6 @@
         ranks - 1 + (span > 0).astype(jnp.int32) + (span < spans - 1).astype(jnp.int32),
     )
 
-    groups = [(h, make) for h in range(heads) for make in (send_pair, send_query)]
-    in_flight = []
-
     def start_group(h, make):
         def step(i, carry):
             make(h, partner(send_step(i))).start()
@@ -153,15 +150,28 @@
 
         lax.fori_loop(0, ranks - 1, step, 0)
 
-    def advance():
-        if groups:
-            if len(in_flight) == 2:
-                drain_group(*in_flight.pop(0))
-            in_flight.append(groups.pop(0))
-            start_group(*in_flight[-1])
-
-    advance()
-    advance()
+    early = span < (spans + 1) // 2
+    late = jnp.logical_not(early)
+    orders = (
+        (early, [(h, make) for make in (send_pair, send_query) for h in range(heads)]),
+        (late, [(h, make) for h in range(heads) for make in (send_query, send_pair)]),
+    )
+    ahead = min(3, 2 * heads)
+    for here, order in orders:
+
+        @pl.when(here)
+        def _(order=order):
+            for group in order[:ahead]:
+                start_group(*group)
+
+    def send_rest(order):
+        for i in range(ahead, 2 * heads):
+            drain_group(*order[i - ahead])
+            start_group(*order[i])
+
+    def drain_rest(order):
+        for group in order[max(0, 2 * heads - ahead) :]:
+            drain_group(*group)
 
     def pass_on(h, j, first, last):
         def step(k, carry):
@@ -177,14 +187,11 @@
         lax.fori_loop(first, last, step, 0)
 
     def pass_near(h):
-        pass_on(h, span, 0, half)
-        advance()
-
         def step(i, carry):
             pass_on(h, span - i, 0, half)
             return carry
 
-        lax.fori_loop(1, span + 1, step, 0)
+        lax.fori_loop(0, span + 1, step, 0)
 
     def pass_far(h, j):
         pass_on(h, j, half, ranks)
@@ -203,8 +210,8 @@
             (((1,), (1,)), ((), ())),
             preferred_element_type=jnp.float32,
         )
-        position = lax.broadcasted_iota(jnp.int32, scores.shape, 1)
-        scores = jnp.where(position < live, scores, MASKED)
+        position = lax.broadcasted_iota(jnp.int32, (1, tokens), 1)
+        scores = jnp.minimum(scores, jnp.where(position < live, -2 * MASKED, MASKED))
         peak = peaks[here, :]
         new_peak = jnp.maximum(peak, jnp.max(scores, axis=1, keepdims=True))
         weights = jnp.exp2((scores - new_peak) * (LOG2E * HD**-0.5)).astype(jnp.bfloat16)
@@ -240,7 +247,7 @@
     def last_block(h):
         def one_tile(tile, carry):
             here = tile_rows(tile)
-            _, total, acc = add_block(h, 0, here, lengths_ref[0])
+            _, total, acc = add_block(h, span, here, lengths_ref[span])
             position = tile * query_tile + lax.broadcasted_iota(jnp.int32, acc.shape, 0)
             value = jnp.where(position < lengths_ref[span], acc / total, 0.0)
             results[h, here, :] = value.astype(jnp.bfloat16)
@@ -267,35 +274,45 @@
 
         lax.fori_loop(0, tiles, one_tile, 0)
 
+    def compute_head(h, waits):
+        wait_queries(h)
+        start_state()
+
+        def step(j, carry):
+            if waits:
+                pass_far(h, j + 1)
+            middle_block(h, j)
+            return carry
+
+        lax.fori_loop(0, span, step, 0)
+        last_block(h)
+
     read_lengths.wait()
-    pass_near(0)
-    for h in range(heads):
-        start_state()
-        pass_far(h, span)
-        advance()
-
-        @pl.when(span > 0)
-        def _(h=h):
-            pass_far(h, span - 1)
-
-        wait_queries(h)
-
-        def step(i, carry, h=h):
-            middle_block(h, span - i)
-
-            @pl.when(i + 1 < span)
-            def _():
-                pass_far(h, span - i - 2)
-
-            return carry
-
-        lax.fori_loop(0, span, step, 0)
-        if h + 1 < heads:
-            pass_near(h + 1)
-        last_block(h)
-
-    for group in in_flight:
-        drain_group(*group)
+
+    @pl.when(early)
+    def _():
+        for h in range(heads):
+            pass_near(h)
+        send_rest(orders[0][1])
+        for h in range(heads):
+
+            def step(i, carry, h=h):
+                pass_far(h, span - i)
+                return carry
+
+            lax.fori_loop(0, span + 1, step, 0)
+        for h in range(heads):
+            compute_head(h, False)
+        drain_rest(orders[0][1])
+
+    @pl.when(late)
+    def _():
+        send_rest(orders[1][1])
+        for h in range(heads):
+            pass_near(h)
+            pass_far(h, 0)
+            compute_head(h, True)
+        drain_rest(orders[1][1])
 
     for h in range(heads):
 

time: 37.8 us -> 39.1 us (1.034)
  Pallas kernels: 36 us -> 37.3 us
    pallas_call x1, Pallas kernels: 36 us -> 37.3 us  [shards(): pl.pallas_call(functools.partial(kernel, spans, ranks, heads, rows), out_...]
where the time goes in v6:
time: 39.1 us; the launch traced here: 39 us
  Pallas kernels  37.3 us (95%)
  local copies, waits for them, and re-layouts  1.67 us (4%)
    pallas_call x1, Pallas kernels, shards(): pl.pallas_call(functools.partial(kernel, spans, ranks, heads, rows), out_...  37.3 us
    unnamed x1, local copies, waits for them, and re-layouts  1.67 us

profile of v6, /device:TPU:5, one launch (start us, length us, event | category | flops | bytes accessed | tf_op | source)
XLA Modules:
  0.0 39.0 jit_solution(10663422611262670721)
XLA Ops:
  0.0 37.3 %shard_map.28 = bf16[1,64,2048]{2,1,0:T(8,128)(2,1)} custom-call(s32[4]{0:T(128)} %lengths_hbm.1, bf16[3,1,64,2048]{3,2,1,0:T(8,128)(2,1)} %qkv_ref.1), custom_call_target="tpu_custom_call" | custom-call | tf_op jit(solution)/shard_map/pallas_call | solution.py:349
  37.3 1.7 %copy.4 = bf16[1,64,2048]{2,1,0:T(8,128)(2,1)} copy(bf16[1,64,2048]{2,1,0:T(8,128)(2,1)} %shard_map.28) | data formatting | bytes 524288

commit v7 on v3

--- a/solution.py
+++ b/solution.py
@@ -15,7 +15,7 @@
 
 def kernel(
     spans, ranks, heads, rows, lengths_hbm, qkv_ref, out_ref,
-    keys, queries, results, peaks, totals, sums, lengths_ref, lengths_sem,
+    keys, queries, results, peaks, sums, lengths_ref, lengths_sem,
     pair_send, query_send, result_send, forward_send,
     pair_recv, query_recv, result_recv,
 ):
@@ -196,76 +196,61 @@
 
         lax.fori_loop(0, ranks, step, 0)
 
-    def add_block(h, j, here, live):
-        scores = lax.dot_general(
-            queries[h, here, :],
-            keys[h, 0, j],
-            (((1,), (1,)), ((), ())),
-            preferred_element_type=jnp.float32,
-        )
-        position = lax.broadcasted_iota(jnp.int32, scores.shape, 1)
-        scores = jnp.where(position < live, scores, MASKED)
-        peak = peaks[here, :]
-        new_peak = jnp.maximum(peak, jnp.max(scores, axis=1, keepdims=True))
-        weights = jnp.exp2((scores - new_peak) * (LOG2E * HD**-0.5)).astype(jnp.bfloat16)
-        scale = jnp.exp2((peak - new_peak) * (LOG2E * HD**-0.5))
-        total = totals[here, :] * scale + jnp.sum(
-            weights.astype(jnp.float32), axis=1, keepdims=True
-        )
-        acc = sums[here, :] * scale + jnp.dot(
-            weights, keys[h, 1, j], preferred_element_type=jnp.float32
-        )
-        return new_peak, total, acc
-
-    def tile_rows(tile):
-        return pl.ds(pl.multiple_of(tile * query_tile, query_tile), query_tile)
-
-    tiles = tokens // query_tile
+    ones = jnp.ones((16, tokens), jnp.bfloat16)
+
+    def add_block(h, j):
+        k = keys[h, 0, j]
+        v = jnp.concatenate([keys[h, 1, j].T, ones], axis=0)
+        live = lax.broadcasted_iota(jnp.int32, (tokens, query_tile), 0) < lengths_ref[j]
+        states = []
+        for first in range(0, tokens, query_tile):
+            here = pl.ds(first, query_tile)
+            scores = lax.dot_general(
+                k,
+                queries[h, here, :],
+                (((1,), (1,)), ((), ())),
+                preferred_element_type=jnp.float32,
+            )
+            scores = jnp.where(live, scores, MASKED)
+            peak = peaks[:, here]
+            new_peak = jnp.maximum(peak, jnp.max(scores, axis=0, keepdims=True))
+            weights = jnp.exp2((scores - new_peak) * (LOG2E * HD**-0.5)).astype(jnp.bfloat16)
+            scale = jnp.exp2((peak - new_peak) * (LOG2E * HD**-0.5))
+            acc = sums[:, here] * scale + jnp.dot(v, weights, preferred_element_type=jnp.float32)
+            states.append((here, new_peak, acc))
+        return states
 
     def start_state():
         peaks[...] = jnp.full(peaks.shape, MASKED, jnp.float32)
-        totals[...] = jnp.zeros(totals.shape, jnp.float32)
         sums[...] = jnp.zeros(sums.shape, jnp.float32)
 
     def middle_block(h, j):
-        def one_tile(tile, carry):
-            here = tile_rows(tile)
-            peaks[here, :], totals[here, :], sums[here, :] = add_block(
-                h, j, here, lengths_ref[j]
-            )
-            return carry
-
-        lax.fori_loop(0, tiles, one_tile, 0)
+        for here, peak, acc in add_block(h, j):
+            peaks[:, here] = peak
+            sums[:, here] = acc
 
     def last_block(h):
-        def one_tile(tile, carry):
-            here = tile_rows(tile)
-            _, total, acc = add_block(h, 0, here, lengths_ref[0])
-            position = tile * query_tile + lax.broadcasted_iota(jnp.int32, acc.shape, 0)
-            value = jnp.where(position < lengths_ref[span], acc / total, 0.0)
-            results[h, here, :] = value.astype(jnp.bfloat16)
-
-            def start_result(i, carry):
-                rank = tile * (query_tile // rows) + i
-
-                @pl.when(rank != me)
-                def _():
-                    send_result(h, rank).start()
-
-                @pl.when(rank == me)
-                def _():
-                    pltpu.make_async_copy(
-                        results.at[h, block_rows(me), :],
-                        out_ref.at[0, :, columns(me, h)],
-                        result_recv.at[h, me],
-                    ).start()
-
-                return carry
-
-            lax.fori_loop(0, query_tile // rows, start_result, 0)
-            return carry
-
-        lax.fori_loop(0, tiles, one_tile, 0)
+        for here, _, acc in add_block(h, 0):
+            position = here.start + lax.broadcasted_iota(jnp.int32, (HD, query_tile), 1)
+            value = jnp.where(position < lengths_ref[span], acc[:HD] / acc[HD : HD + 1], 0.0)
+            results[h, here, :] = value.T.astype(jnp.bfloat16)
+
+        def start_result(rank, carry):
+            @pl.when(rank != me)
+            def _():
+                send_result(h, rank).start()
+
+            @pl.when(rank == me)
+            def _():
+                pltpu.make_async_copy(
+                    results.at[h, block_rows(me), :],
+                    out_ref.at[0, :, columns(me, h)],
+                    result_recv.at[h, me],
+                ).start()
+
+            return carry
+
+        lax.fori_loop(0, ranks, start_result, 0)
 
     read_lengths.wait()
     pass_near(0)
@@ -341,9 +326,8 @@
             pltpu.VMEM((heads, 2, spans, tokens, HD), jnp.bfloat16),
             pltpu.VMEM((heads, tokens, HD), jnp.bfloat16),
             pltpu.VMEM((heads, tokens, HD), jnp.bfloat16),
-            pltpu.VMEM((tokens, 1), jnp.float32),
-            pltpu.VMEM((tokens, 1), jnp.float32),
-            pltpu.VMEM((tokens, HD), jnp.float32),
+            pltpu.VMEM((1, tokens), jnp.float32),
+            pltpu.VMEM((HD + 16, tokens), jnp.float32),
             pltpu.SMEM((spans,), jnp.int32),
             dma(()),
             dma((heads, ranks)),

time: 37.8 us -> 37.8 us (level)
  no operation moved by 1% of the time
where the time goes in v7:
time: 37.8 us; the launch traced here: 37.6 us
  Pallas kernels  35.9 us (95%)
  local copies, waits for them, and re-layouts  1.67 us (4%)
    pallas_call x1, Pallas kernels, shards(): pl.pallas_call(functools.partial(kernel, spans, ranks, heads, rows), out_...  35.9 us
    unnamed x1, local copies, waits for them, and re-layouts  1.67 us

profile of v7, /device:TPU:5, one launch (start us, length us, event | category | flops | bytes accessed | tf_op | source)
XLA Modules:
  0.0 37.6 jit_solution(10086956246002366997)
XLA Ops:
  0.0 35.9 %shard_map.28 = bf16[1,64,2048]{2,1,0:T(8,128)(2,1)} custom-call(s32[4]{0:T(128)} %lengths_hbm.1, bf16[3,1,64,2048]{3,2,1,0:T(8,128)(2,1)} %qkv_ref.1), custom_call_target="tpu_custom_call" | custom-call | tf_op jit(solution)/shard_map/pallas_call | solution.py:317
  36.0 1.7 %copy.4 = bf16[1,64,2048]{2,1,0:T(8,128)(2,1)} copy(bf16[1,64,2048]{2,1,0:T(8,128)(2,1)} %shard_map.28) | data formatting | bytes 524288

commit v8 on v7

--- a/solution.py
+++ b/solution.py
@@ -136,9 +136,6 @@
         ranks - 1 + (span > 0).astype(jnp.int32) + (span < spans - 1).astype(jnp.int32),
     )
 
-    groups = [(h, make) for h in range(heads) for make in (send_pair, send_query)]
-    in_flight = []
-
     def start_group(h, make):
         def step(i, carry):
             make(h, partner(send_step(i))).start()
@@ -153,15 +150,28 @@
 
         lax.fori_loop(0, ranks - 1, step, 0)
 
-    def advance():
-        if groups:
-            if len(in_flight) == 2:
-                drain_group(*in_flight.pop(0))
-            in_flight.append(groups.pop(0))
-            start_group(*in_flight[-1])
-
-    advance()
-    advance()
+    early = span < (spans + 1) // 2
+    late = jnp.logical_not(early)
+    orders = (
+        (early, [(h, make) for make in (send_pair, send_query) for h in range(heads)]),
+        (late, [(h, make) for h in range(heads) for make in (send_query, send_pair)]),
+    )
+    ahead = min(3, 2 * heads)
+    for here, order in orders:
+
+        @pl.when(here)
+        def _(order=order):
+            for group in order[:ahead]:
+                start_group(*group)
+
+    def send_rest(order):
+        for i in range(ahead, 2 * heads):
+            drain_group(*order[i - ahead])
+            start_group(*order[i])
+
+    def drain_rest(order):
+        for group in order[max(0, 2 * heads - ahead) :]:
+            drain_group(*group)
 
     def pass_on(h, j, first, last):
         def step(k, carry):
@@ -177,14 +187,11 @@
         lax.fori_loop(first, last, step, 0)
 
     def pass_near(h):
-        pass_on(h, span, 0, half)
-        advance()
-
         def step(i, carry):
             pass_on(h, span - i, 0, half)
             return carry
 
-        lax.fori_loop(1, span + 1, step, 0)
+        lax.fori_loop(0, span + 1, step, 0)
 
     def pass_far(h, j):
         pass_on(h, j, half, ranks)
@@ -230,7 +237,7 @@
             sums[:, here] = acc
 
     def last_block(h):
-        for here, _, acc in add_block(h, 0):
+        for here, _, acc in add_block(h, span):
             position = here.start + lax.broadcasted_iota(jnp.int32, (HD, query_tile), 1)
             value = jnp.where(position < lengths_ref[span], acc[:HD] / acc[HD : HD + 1], 0.0)
             results[h, here, :] = value.T.astype(jnp.bfloat16)
@@ -252,35 +259,45 @@
 
         lax.fori_loop(0, ranks, start_result, 0)
 
+    def compute_head(h, waits):
+        wait_queries(h)
+        start_state()
+
+        def step(j, carry):
+            if waits:
+                pass_far(h, j + 1)
+            middle_block(h, j)
+            return carry
+
+        lax.fori_loop(0, span, step, 0)
+        last_block(h)
+
     read_lengths.wait()
-    pass_near(0)
-    for h in range(heads):
-        start_state()
-        pass_far(h, span)
-        advance()
-
-        @pl.when(span > 0)
-        def _(h=h):
-            pass_far(h, span - 1)
-
-        wait_queries(h)
-
-        def step(i, carry, h=h):
-            middle_block(h, span - i)
-
-            @pl.when(i + 1 < span)
-            def _():
-                pass_far(h, span - i - 2)
-
-            return carry
-
-        lax.fori_loop(0, span, step, 0)
-        if h + 1 < heads:
-            pass_near(h + 1)
-        last_block(h)
-
-    for group in in_flight:
-        drain_group(*group)
+
+    @pl.when(early)
+    def _():
+        for h in range(heads):
+            pass_near(h)
+        send_rest(orders[0][1])
+        for h in range(heads):
+
+            def step(i, carry, h=h):
+                pass_far(h, span - i)
+                return carry
+
+            lax.fori_loop(0, span + 1, step, 0)
+        for h in range(heads):
+            compute_head(h, False)
+        drain_rest(orders[0][1])
+
+    @pl.when(late)
+    def _():
+        send_rest(orders[1][1])
+        for h in range(heads):
+            pass_near(h)
+            pass_far(h, 0)
+            compute_head(h, True)
+        drain_rest(orders[1][1])
 
     for h in range(heads):
 

time: 37.8 us -> 38.3 us (1.013)
  Pallas kernels: 35.9 us -> 36.5 us
    pallas_call x1, Pallas kernels: 35.9 us -> 36.5 us  [shards(): pl.pallas_call(functools.partial(kernel, spans, ranks, heads, rows), out_...]
where the time goes in v8:
time: 38.3 us; the launch traced here: 38.2 us
  Pallas kernels  36.5 us (95%)
  local copies, waits for them, and re-layouts  1.67 us (4%)
    pallas_call x1, Pallas kernels, shards(): pl.pallas_call(functools.partial(kernel, spans, ranks, heads, rows), out_...  36.5 us
    unnamed x1, local copies, waits for them, and re-layouts  1.67 us

profile of v8, /device:TPU:5, one launch (start us, length us, event | category | flops | bytes accessed | tf_op | source)
XLA Modules:
  0.0 38.2 jit_solution(3806613752665657100)
XLA Ops:
  0.0 36.5 %shard_map.28 = bf16[1,64,2048]{2,1,0:T(8,128)(2,1)} custom-call(s32[4]{0:T(128)} %lengths_hbm.1, bf16[3,1,64,2048]{3,2,1,0:T(8,128)(2,1)} %qkv_ref.1), custom_call_target="tpu_custom_call" | custom-call | tf_op jit(solution)/shard_map/pallas_call | solution.py:334
  36.5 1.7 %copy.4 = bf16[1,64,2048]{2,1,0:T(8,128)(2,1)} copy(bf16[1,64,2048]{2,1,0:T(8,128)(2,1)} %shard_map.28) | data formatting | bytes 524288

commit v9 on v8

--- a/solution.py
+++ b/solution.py
@@ -152,6 +152,7 @@
 
     early = span < (spans + 1) // 2
     late = jnp.logical_not(early)
+    last = span == spans - 1
     orders = (
         (early, [(h, make) for make in (send_pair, send_query) for h in range(heads)]),
         (late, [(h, make) for h in range(heads) for make in (send_query, send_pair)]),
@@ -265,7 +266,11 @@
 
         def step(j, carry):
             if waits:
-                pass_far(h, j + 1)
+
+                @pl.when(last)
+                def _():
+                    pass_far(h, j + 1)
+
             middle_block(h, j)
             return carry
 
@@ -293,9 +298,25 @@
     @pl.when(late)
     def _():
         send_rest(orders[1][1])
+
+        @pl.when(jnp.logical_not(last))
+        def _():
+            for h in range(heads):
+                pass_near(h)
+
+                def step(j, carry, h=h):
+                    pass_far(h, j)
+                    return carry
+
+                lax.fori_loop(0, span + 1, step, 0)
+
         for h in range(heads):
-            pass_near(h)
-            pass_far(h, 0)
+
+            @pl.when(last)
+            def _(h=h):
+                pass_near(h)
+                pass_far(h, 0)
+
             compute_head(h, True)
         drain_rest(orders[1][1])
 

time: 38.3 us -> 38.6 us (level)
  no operation moved by 1% of the time
where the time goes in v9:
time: 38.6 us; the launch traced here: 38.4 us
  Pallas kernels  36.8 us (95%)
  local copies, waits for them, and re-layouts  1.67 us (4%)
    pallas_call x1, Pallas kernels, shards(): pl.pallas_call(functools.partial(kernel, spans, ranks, heads, rows), out_...  36.8 us
    unnamed x1, local copies, waits for them, and re-layouts  1.67 us

profile of v9, /device:TPU:5, one launch (start us, length us, event | category | flops | bytes accessed | tf_op | source)
XLA Modules:
  0.0 38.4 jit_solution(1540050254807126148)
XLA Ops:
  0.0 36.8 %shard_map.28 = bf16[1,64,2048]{2,1,0:T(8,128)(2,1)} custom-call(s32[4]{0:T(128)} %lengths_hbm.1, bf16[3,1,64,2048]{3,2,1,0:T(8,128)(2,1)} %qkv_ref.1), custom_call_target="tpu_custom_call" | custom-call | tf_op jit(solution)/shard_map/pallas_call | solution.py:355
  36.8 1.7 %copy.4 = bf16[1,64,2048]{2,1,0:T(8,128)(2,1)} copy(bf16[1,64,2048]{2,1,0:T(8,128)(2,1)} %shard_map.28) | data formatting | bytes 524288

commit v10 on v7

--- a/solution.py
+++ b/solution.py
@@ -177,14 +177,12 @@
         lax.fori_loop(first, last, step, 0)
 
     def pass_near(h):
-        pass_on(h, span, 0, half)
-        advance()
-
         def step(i, carry):
             pass_on(h, span - i, 0, half)
             return carry
 
-        lax.fori_loop(1, span + 1, step, 0)
+        lax.fori_loop(0, span + 1, step, 0)
+        advance()
 
     def pass_far(h, j):
         pass_on(h, j, half, ranks)
@@ -257,12 +255,12 @@
     for h in range(heads):
         start_state()
         pass_far(h, span)
-        advance()
 
         @pl.when(span > 0)
         def _(h=h):
             pass_far(h, span - 1)
 
+        advance()
         wait_queries(h)
 
         def step(i, carry, h=h):

time: 37.8 us -> 37.7 us (level)
  no operation moved by 1% of the time
where the time goes in v10:
time: 37.7 us; the launch traced here: 37.5 us
  Pallas kernels  35.8 us (95%)
  local copies, waits for them, and re-layouts  1.67 us (4%)
    pallas_call x1, Pallas kernels, shards(): pl.pallas_call(functools.partial(kernel, spans, ranks, heads, rows), out_...  35.8 us
    unnamed x1, local copies, waits for them, and re-layouts  1.67 us

profile of v10, /device:TPU:5, one launch (start us, length us, event | category | flops | bytes accessed | tf_op | source)
XLA Modules:
  0.0 37.5 jit_solution(4150781019003522830)
XLA Ops:
  0.0 35.8 %shard_map.28 = bf16[1,64,2048]{2,1,0:T(8,128)(2,1)} custom-call(s32[4]{0:T(128)} %lengths_hbm.1, bf16[3,1,64,2048]{3,2,1,0:T(8,128)(2,1)} %qkv_ref.1), custom_call_target="tpu_custom_call" | custom-call | tf_op jit(solution)/shard_map/pallas_call | solution.py:315
  35.8 1.7 %copy.4 = bf16[1,64,2048]{2,1,0:T(8,128)(2,1)} copy(bf16[1,64,2048]{2,1,0:T(8,128)(2,1)} %shard_map.28) | data formatting | bytes 524288
